TPU v7x, 32 devices: a whole 2x2x4 slice. The times are simulated.
32 devices in a mesh: groups: 2 (over y), ctx: 8 (over z, x), head: 2 (over core).
Axes of the slice: x: 2, y: 2, z: 4, core: 2. Of those that a mesh axis runs over, the one named last changes fastest.
Arguments:
- queries: bfloat16 [8192, 2048], P(('groups', 'ctx'), 'head'), parts along dimension 0, may hold values from -90 to 90
- keys: bfloat16 [8192, 2048], P(('groups', 'ctx'), 'head'), parts along dimension 0, may hold values from -7 to 7
- values: bfloat16 [8192, 2048], P(('groups', 'ctx'), 'head'), parts along dimension 0, may hold values from -6 to 6
- rates: float32 [4, 8192], P('head', ('groups', 'ctx')), parts along dimension 1, may hold values from 0.01 to 0.1
- windows: int32 [8], P(('groups', 'head')), parts along dimension 0, may hold values from 512 to 1024, as said below
- counts: int32 [16], P(('groups', 'ctx')), parts along dimension 0, may hold values from 128 to 512, as said below
- fast: bfloat16 [256, 4, 3, 512], P(None, 'head'), may hold values from -0.25 to 0.25
Outputs:
- mixed: bfloat16 [8192, 2048], P(('groups', 'ctx'), 'head'), parts along dimension 0
- new_fast: bfloat16 [512, 4, 3, 512], P(('groups', 'ctx'), 'head'), parts along dimension 0
There are 2 independent parts, one for each index of `groups`. A program takes and returns all parts, laid end to end along the dimension named above; an argument that names none is the same for every part. Nothing has to cross between parts.
Inputs may be any that keep to these rules, and one draw needn't show every extreme that they name: `windows`: some head's window is exactly 1024. `counts`: some shard is full.
All inputs are finite; a program needn't handle non-finite values.
Results may differ from a plain program's by a relative error of at most 0.0065.
Values may be sent and summed in bfloat16 or wider, within the bound.
A program may use at most 128 MiB of HBM per device.

v0:
```python
import jax
import jax.numpy as jnp
from jax import lax
from jax.sharding import PartitionSpec as P

ATTENTION_SPAN = 1024


def passed_along(x, axis, by):
    devices = lax.axis_size(axis)
    pairs = [(i, i + by) for i in range(devices) if 0 <= i + by < devices]
    return lax.ppermute(x, axis, pairs)


def normalise(upd, width):
    scale = lax.rsqrt(jnp.mean(upd * upd, axis=-1, keepdims=True) + 1e-06) * width ** (-0.5)
    return (upd * scale).astype(jnp.bfloat16)


def on_device(queries, keys, values, rates, windows, counts, fast):
    tok = queries.shape[0]
    fh = fast.shape[0]
    heads_here = fast.shape[1]
    dh = fast.shape[3]
    length = tok * lax.axis_size("ctx")
    ctx_index = lax.axis_index("ctx")
    local_pos = jnp.arange(tok, dtype=jnp.int32)
    valid = local_pos < counts[0]
    validf = valid.astype(jnp.float32)
    q_heads = queries.reshape(tok, heads_here, dh)
    k_heads = keys.reshape(tok, heads_here, dh)
    v_heads = values.reshape(tok, heads_here, dh)
    h1 = jnp.einsum("thd,fhd->thf", k_heads, fast[:, :, 0], preferred_element_type=jnp.float32)
    h3 = jnp.einsum("thd,fhd->thf", k_heads, fast[:, :, 2], preferred_element_type=jnp.float32)
    dg = jnp.einsum("thd,fhd->thf", v_heads, fast[:, :, 1], preferred_element_type=jnp.float32)
    coef = (rates.T * validf[:, None])[:, :, None]
    sig = jax.nn.sigmoid(h1)
    dh1 = (-coef * dg * h3 * sig * (1.0 + h1 * (1.0 - sig))).astype(jnp.bfloat16)
    dh3 = (-coef * dg * h1 * sig).astype(jnp.bfloat16)
    e_two = (-coef * h1 * sig * h3).astype(jnp.bfloat16)
    rows_own = fh // lax.axis_size("ctx")
    own_start = ctx_index * rows_own
    g_one = jnp.einsum("thf,thd->fhd", dh1, k_heads, preferred_element_type=jnp.float32)
    g_two = jnp.einsum("thf,thd->fhd", e_two, v_heads, preferred_element_type=jnp.float32)
    g_three = jnp.einsum("thf,thd->fhd", dh3, k_heads, preferred_element_type=jnp.float32)
    grads = lax.psum(jnp.stack([g_one, g_two, g_three], axis=2), "ctx")
    new_full = normalise(fast.astype(jnp.float32) - grads * length ** (-0.5), dh)
    new_own = lax.dynamic_slice_in_dim(new_full, own_start, rows_own, 0)
    a_one = jnp.einsum(
        "thd,fhd->thf", q_heads, new_full[:, :, 0], preferred_element_type=jnp.float32
    )
    a_three = jnp.einsum(
        "thd,fhd->thf", q_heads, new_full[:, :, 2], preferred_element_type=jnp.float32
    )
    gated = (jax.nn.silu(a_one) * a_three).astype(jnp.bfloat16)
    ttt = jnp.einsum(
        "thf,fhd->thd", gated, new_full[:, :, 1], preferred_element_type=jnp.float32
    ) * fh ** (-0.5)
    all_counts = lax.all_gather(counts, "ctx", axis=0, tiled=True)
    span = ATTENTION_SPAN // tok
    pieces = []
    carried = (keys, values)
    for step in range(span):
        carried = passed_along((carried[0], carried[1]), "ctx", 1)
        pieces.append(carried)
    key_list = [pieces[span - 1 - index][0] for index in range(span)] + [keys]
    value_list = [pieces[span - 1 - index][1] for index in range(span)] + [values]
    near_keys = jnp.concatenate(key_list, axis=0).reshape((span + 1) * tok, heads_here, dh)
    near_values = jnp.concatenate(value_list, axis=0).reshape((span + 1) * tok, heads_here, dh)
    source = ctx_index - span + jnp.arange(span + 1, dtype=jnp.int32)
    source_count = jnp.where(source >= 0, all_counts[jnp.clip(source, 0, None)], 0)
    key_valid = (local_pos[None, :] < source_count[:, None]).reshape((span + 1) * tok)
    key_pos = (source[:, None] * tok + local_pos[None, :]).reshape((span + 1) * tok)
    query_pos = ctx_index * tok + local_pos
    diff = query_pos[:, None] - key_pos[None, :]
    allowed = (
        (diff[None] >= 0)
        & (diff[None] < windows[:, None, None])
        & (key_valid[None, None, :] | (diff[None] == 0))
    )
    scores = jnp.einsum(
        "thd,khd->htk", q_heads, near_keys, preferred_element_type=jnp.float32
    ) * dh ** (-0.5)
    scores = jnp.where(allowed, scores, -1e30)
    top = jnp.max(scores, axis=2, keepdims=True)
    weights = jnp.where(allowed, jnp.exp(scores - top), 0.0)
    probs = (weights / jnp.sum(weights, axis=2, keepdims=True)).astype(jnp.bfloat16)
    attn = jnp.einsum("htk,khd->thd", probs, near_values, preferred_element_type=jnp.float32)
    mixed = (
        (validf[:, None, None] * (attn + ttt)).astype(jnp.bfloat16).reshape(tok, heads_here * dh)
    )
    return (mixed, new_own)


def solution(mesh):
    in_specs = (
        P(("groups", "ctx"), "head"),
        P(("groups", "ctx"), "head"),
        P(("groups", "ctx"), "head"),
        P("head", ("groups", "ctx")),
        P(("groups", "head")),
        P(("groups", "ctx")),
        P(None, "head", None, None),
    )
    out_specs = (P(("groups", "ctx"), "head"), P(("groups", "ctx"), "head", None, None))
    return jax.shard_map(
        on_device, mesh=mesh, in_specs=in_specs, out_specs=out_specs, check_vma=False
    )
```

profile of v0, /device:TPU:28, one launch (start us, length us, event | category | flops | bytes accessed | tf_op | source)
XLA Modules:
  0.0 213.8 jit_solution(2257052703852368711)
XLA Ops:
  7.2 0.0 copy-start.2
  7.2 0.0 all-reduce.3.cloned.1.call-start
  7.2 3.5 %collective-permute-start = (bf16[512,1024]{1,0:T(8,128)(2,1)}, bf16[512,1024]{1,0:T(8,128)(2,1)}, u32[]{:S(2)}, u32[]{:S(2)}) collective-permute-start(bf16[512,1024]{1,0:T(8,128)(2,1)} %param.9), channel_id=1, source_target_pairs={{0,2},{2,4},{4,6},{6,8},{8,10},{10,12},{12,14},{1,3},{3,5},{5,7},{... | collective-permute-start | bytes 3145736 | tf_op jit(solution)/shard_map/ppermute | solution.py:12
  10.8 1.7 copy.33
  12.4 0.0 copy-start.9
  12.5 0.0 copy-start.7
  12.5 0.0 copy-done.2
  12.5 0.5 convolution_bitcast_fusion.5
  13.0 0.5 convolution_bitcast_fusion.6
  14.1 0.0 copy-done.9
  14.2 0.0 copy-done.7
  14.2 0.5 fusion.10
  14.6 0.5 convolution_bitcast_fusion.3
  15.2 0.6 convolution_bitcast_fusion.4
  15.7 0.5 convolution_bitcast_fusion.2
  16.2 2.0 pad_maximum_fusion.2
  18.2 0.0 copy-start.11
  18.2 0.0 all-reduce.3.cloned.1.call-update
  18.2 0.0 copy-start.6
  18.2 0.5 copy.28
  18.8 0.0 copy-start.4
  18.8 0.0 copy-done.11
  18.8 0.7 dynamic-slice
  19.5 0.8 dynamic-update-slice
  20.3 1.9 collective-permute-start.2
  22.2 45.0 %all-reduce = s32[8]{0:T(128)S(1)} all-reduce(s32[8]{0:T(128)S(1)} %dynamic-update-slice), channel_id=1, replica_groups=mesh['groups'=2,'ctx'=8,'head'=2] {'ctx'}, use_global_device_ids=true, to_apply=%add | all-reduce | flops 8 | bytes 64
  67.2 0.6 gather_fusion
  67.8 0.1 iota_add_fusion
  67.9 0.0 collective-permute-done
  67.9 28.2 %collective-permute-start.1 = (bf16[512,1024]{1,0:T(8,128)(2,1)}, bf16[512,1024]{1,0:T(8,128)(2,1)}, u32[]{:S(2)}, u32[]{:S(2)}) collective-permute-start(bf16[512,1024]{1,0:T(8,128)(2,1)} %collective-permute-done), channel_id=1, source_target_pairs={{0,2},{2,4},{4,6},{6,8},{8,10},{10,12},{12,14},{1,3},{3,5},{5,7},{... | collective-permute-start | bytes 3145736 | tf_op jit(solution)/shard_map/ppermute | solution.py:12
  96.1 1.9 broadcast_subtract_fusion
  98.1 0.0 copy-done.6
  98.1 1.3 copy.53
  99.4 0.0 collective-permute-done.2
  99.4 2.1 collective-permute-start.3
  101.5 0.1 iota_compare_fusion
  101.6 2.2 %subtract_compare_fusion = (pred[512,1536]{0,1:T(8,128)(4,1)}, pred[512,1536]{0,1:T(8,128)(4,1)}) fusion(s32[1536]{0:T(1024)S(1)} %add.94, s32[512]{0:T(512)S(1)} %iota_add_fusion.1, pred[1536]{0:T(1024)(128)(4,1)S(1)} %lt.56), kind=kLoop, calls=%fused_computation.21 | loop fusion | flops 3145728 | bytes 1582592 | tf_op jit(solution)/shard_map/ge | solution.py:77
  103.8 0.0 copy-done.4
  103.8 22.9 %collective-permute-done.1 = bf16[512,1024]{1,0:T(8,128)(2,1)} collective-permute-done((bf16[512,1024]{1,0:T(8,128)(2,1)}, bf16[512,1024]{1,0:T(8,128)(2,1)}, u32[]{:S(2)}, u32[]{:S(2)}) %collective-permute-start.1) | collective-permute-done | bytes 1048608 | tf_op jit(solution)/shard_map/ppermute | solution.py:12
  126.7 2.2 %pad_maximum_fusion = bf16[1536,1024]{1,0:T(8,128)(2,1)S(1)} fusion(bf16[512,1024]{1,0:T(8,128)(2,1)} %param.9, bf16[512,1024]{1,0:T(8,128)(2,1)} %collective-permute-done, bf16[512,1024]{1,0:T(8,128)(2,1)} %collective-permute-done.1), kind=kLoop, calls=%fused_computation.7 | loop fusion | flops 9437184 | bytes 6291456 | tf_op jit(solution)/shard_map/concatenate | solution.py:69
  128.9 3.0 %copy.27 = bf16[1536,1024]{0,1:T(8,128)(2,1)} copy(bf16[1536,1024]{1,0:T(8,128)(2,1)S(1)} %pad_maximum_fusion) | data formatting | bytes 6291456 | tf_op jit(solution)/shard_map/concatenate | solution.py:69
  131.9 0.0 copy-start.3
  131.9 0.0 copy-start.8
  131.9 0.0 copy-start.10
  131.9 23.8 %collective-permute-done.3 = bf16[512,1024]{0,1:T(8,128)(2,1)} collective-permute-done((bf16[512,1024]{0,1:T(8,128)(2,1)}, bf16[512,1024]{0,1:T(8,128)(2,1)}, u32[]{:S(2)}, u32[]{:S(2)}) %collective-permute-start.3) | collective-permute-done | bytes 1048608 | tf_op jit(solution)/shard_map/ppermute | solution.py:12
  155.7 3.2 %pad_maximum_fusion.1 = bf16[1536,1024]{0,1:T(8,128)(2,1)} fusion(bf16[512,1024]{0,1:T(8,128)(2,1)} %copy-done.4, bf16[512,1024]{0,1:T(8,128)(2,1)} %collective-permute-done.2, bf16[512,1024]{0,1:T(8,128)(2,1)} %collective-permute-done.3), kind=kLoop, calls=%fused_computation.8 | loop fusion | flops 9437184 | bytes 6291456 | tf_op jit(solution)/shard_map/concatenate | solution.py:68
  158.9 0.0 copy-done.3
  158.9 0.0 copy-done.8
  158.9 0.0 copy-done.10
  158.9 0.0 copy-start
  158.9 12.9 %fusion.43 = (f32[2,512]{1,0:T(2,128)S(1)}, f32[2,512,1536]{1,2,0:T(8,128)}) fusion(s32[512,1536]{0,1:T(8,128)} %broadcast_subtract_fusion, s32[2]{0:T(128)S(1)} %copy-done.10, pred[512,1536]{0,1:T(8,128)(4,1)} %get-tuple-element.7, pred[512,1536]{0,1:T(8,128)(4,1)S(1)} %copy-done.8, bf16[1536,2,512]{0,2,1:T(8,128)(2,1)} %bitcast.98, ...), kind=kOutput, calls=%fused_computation.87 | convolution fusion | flops 1627915776 | bytes 15208456 | tf_op jit(solution)/shard_map/sub | solution.py:86
  171.9 17.5 %all-reduce.3.cloned.1.call-done = f32[256,2,3,512]{3,0,1,2:T(8,128)} async-done(((f32[256,2,3,512]{3,0,1,2:T(8,128)}), f32[256,2,3,512]{3,0,1,2:T(8,128)}) %all-reduce.3.cloned.1.call-update) | async-done | bytes 3145744 | tf_op jit(solution)/shard_map/psum | solution.py:46
  189.3 0.0 copy-done
  189.3 2.6 %multiply_reduce_fusion = f32[256,2,3]{0,1,2:T(2,128)S(1)} fusion(f32[256,2,3,512]{3,0,1,2:T(8,128)} %all-reduce.3.cloned.1.call-done, bf16[256,2,3,512]{3,1,2,0:T(2,128)(2,1)S(1)} %copy-done), kind=kLoop, calls=%fused_computation.11 | loop fusion | flops 3930624 | bytes 4724736 | tf_op jit(solution)/shard_map/reduce_sum | solution.py:16
  192.0 0.2 copy-done.1
  192.2 0.5 multiply_convert_fusion
  192.6 0.0 copy-start.5
  192.7 1.2 copy-done.5
  193.9 0.4 convolution_bitcast_fusion.1
  194.3 3.4 %fusion.12 = f32[2,512,512]{2,1,0:T(8,128)} fusion(bf16[512,2,512]{0,2,1:T(8,128)(2,1)S(1)} %bitcast.96, f32[512,2,256]{0,2,1:T(8,128)S(1)} %convolution_bitcast_fusion.1, bf16[256,2,3,512]{3,0,1,2:T(8,128)(2,1)} %copy-done.5), kind=kOutput, calls=%fused_computation.35 | convolution fusion | flops 538443776 | bytes 5242880 | tf_op jit(solution)/shard_map/thf,fhd->thd/dot_general | solution.py:56
  197.7 6.1 %multiply_convert_fusion.1 = bf16[2,512,512]{2,1,0:T(8,128)(2,1)S(1)} fusion(f32[2,512,512]{2,1,0:T(8,128)} %fusion.12, bf16[1536,2,512]{0,2,1:T(8,128)(2,1)} %bitcast.97, f32[2,512,1536]{1,2,0:T(8,128)} %get-tuple-element.9, f32[2,512]{1,0:T(2,128)S(1)} %get-tuple-element.8, f32[512]{0:T(512)S(1)} %fusion.35), kind=kOutput, calls=%fused_computation.22 | convolution fusion | flops 1615855616 | bytes 12589056 | tf_op jit(solution)/shard_map/htk,khd->thd/dot_general | solution.py:88
  203.8 1.3 copy.46
  205.1 0.9 constant_dynamic-slice_fusion
  206.1 0.9 copy.47
  (11 shorter events, 0.1 us)
Async XLA Ops:
  7.2 5.3 %copy-start.2 = (bf16[512,1024]{1,0:T(8,128)(2,1)S(1)}, bf16[512,1024]{1,0:T(8,128)(2,1)}, u32[]{:S(2)}) copy-start(bf16[512,1024]{1,0:T(8,128)(2,1)} %param.8) | copy-start | bytes 3145732
  7.2 182.2 %all-reduce.3.cloned.1.call-start = ((), (), s32[]{:S(2)}) async-start(), calls=%async_computation | async-start | bytes 6291456 | tf_op jit(solution)/shard_map/psum | solution.py:46
  7.2 60.7 %collective-permute-start = (bf16[512,1024]{1,0:T(8,128)(2,1)}, bf16[512,1024]{1,0:T(8,128)(2,1)}, u32[]{:S(2)}, u32[]{:S(2)}) collective-permute-start(bf16[512,1024]{1,0:T(8,128)(2,1)} %param.9), channel_id=1, source_target_pairs={{0,2},{2,4},{4,6},{6,8},{8,10},{10,12},{12,14},{1,3},{3,5},{5,7},{... | collective-permute-start | bytes 3145736 | tf_op jit(solution)/shard_map/ppermute | solution.py:12
  12.4 1.7 copy-start.9
  12.5 1.7 copy-start.7
  18.2 0.7 copy-start.11
  18.2 79.9 %copy-start.6 = (bf16[512,1024]{1,0:T(8,128)(2,1)S(1)}, bf16[512,1024]{1,0:T(8,128)(2,1)}, u32[]{:S(2)}) copy-start(bf16[512,1024]{1,0:T(8,128)(2,1)} %param.7) | copy-start | bytes 3145732
  18.8 85.0 %copy-start.4 = (bf16[512,1024]{0,1:T(8,128)(2,1)}, bf16[512,1024]{0,1:T(8,128)(2,1)S(1)}, u32[]{:S(2)}) copy-start(bf16[512,1024]{0,1:T(8,128)(2,1)S(1)} %copy.28) | copy-start | bytes 3145732
  20.3 79.1 %collective-permute-start.2 = (bf16[512,1024]{0,1:T(8,128)(2,1)S(1)}, bf16[512,1024]{0,1:T(8,128)(2,1)}, u32[]{:S(2)}, u32[]{:S(2)}) collective-permute-start(bf16[512,1024]{0,1:T(8,128)(2,1)S(1)} %copy.28), channel_id=1, source_target_pairs={{0,2},{2,4},{4,6},{6,8},{8,10},{10,12},{12,14},{1,3},{3,5},{5,7},{... | collective-permute-start | bytes 3145736 | tf_op jit(solution)/shard_map/ppermute | solution.py:12
  67.9 58.8 %collective-permute-start.1 = (bf16[512,1024]{1,0:T(8,128)(2,1)}, bf16[512,1024]{1,0:T(8,128)(2,1)}, u32[]{:S(2)}, u32[]{:S(2)}) collective-permute-start(bf16[512,1024]{1,0:T(8,128)(2,1)} %collective-permute-done), channel_id=1, source_target_pairs={{0,2},{2,4},{4,6},{6,8},{8,10},{10,12},{12,14},{1,3},{3,5},{5,7},{... | collective-permute-start | bytes 3145736 | tf_op jit(solution)/shard_map/ppermute | solution.py:12
  99.4 56.3 %collective-permute-start.3 = (bf16[512,1024]{0,1:T(8,128)(2,1)}, bf16[512,1024]{0,1:T(8,128)(2,1)}, u32[]{:S(2)}, u32[]{:S(2)}) collective-permute-start(bf16[512,1024]{0,1:T(8,128)(2,1)} %collective-permute-done.2), channel_id=1, source_target_pairs={{0,2},{2,4},{4,6},{6,8},{8,10},{10,12},{12,14},{1,3},{3,5},{5,7},{... | collective-permute-start | bytes 3145736 | tf_op jit(solution)/shard_map/ppermute | solution.py:12
  131.9 27.0 %copy-start.3 = (bf16[512,1024]{0,1:T(8,128)(2,1)S(1)}, bf16[512,1024]{0,1:T(8,128)(2,1)}, u32[]{:S(2)}) copy-start(bf16[512,1024]{0,1:T(8,128)(2,1)} %copy.53) | copy-start | bytes 3145732
  131.9 27.0 %copy-start.8 = (pred[512,1536]{0,1:T(8,128)(4,1)S(1)}, pred[512,1536]{0,1:T(8,128)(4,1)}, u32[]{:S(2)}) copy-start(pred[512,1536]{0,1:T(8,128)(4,1)} %get-tuple-element.6) | copy-start | bytes 2359300
  131.9 27.0 %copy-start.10 = (s32[2]{0:T(128)S(1)}, s32[2]{0:T(128)}, u32[]{:S(2)}) copy-start(s32[2]{0:T(128)} %param.11) | copy-start | bytes 28
  158.9 30.4 %copy-start = (bf16[256,2,3,512]{3,1,2,0:T(2,128)(2,1)S(1)}, bf16[256,2,3,512]{3,1,2,0:T(2,128)(2,1)}, u32[]{:S(2)}) copy-start(bf16[256,2,3,512]{3,1,2,0:T(2,128)(2,1)} %param.13) | copy-start | bytes 4718596
  189.3 2.8 %copy-start.1 = (f32[256,2,3,512]{3,0,1,2:T(8,128)S(1)}, f32[256,2,3,512]{3,0,1,2:T(8,128)}, u32[]{:S(2)}) copy-start(f32[256,2,3,512]{3,0,1,2:T(8,128)} %all-reduce.3.cloned.1.call-done) | copy-start | bytes 9437188
  192.6 1.2 copy-start.5
Sparse Core Ops, SparseCore 0:
  18.3 170.9 all-reduce.2
where the time goes:
time: 218 us; the launch traced here: 214 us
  waiting for transfers between devices  64.2 us (29%)
  blocking collectives  45 us (21%)
  starting transfers between devices  35.8 us (16%)
  matrix products  25.9 us (12%)
  between operations  14.9 us (7%)
  other arithmetic  14.8 us (7%)
  local copies, waits for them, and re-layouts  13.3 us (6%)
    ppermute x4, waiting for transfers between devices, passed_along(): return lax.ppermute(x, axis, pairs)  46.7 us
    unnamed x1, blocking collectives  45 us
    ppermute x4, starting transfers between devices, passed_along(): return lax.ppermute(x, axis, pairs)  35.7 us
    psum x1, waiting for transfers between devices, on_device(): grads = lax.psum(jnp.stack([g_one, g_two, g_three], axis=2), 'ctx')  17.5 us
    sub x1, matrix products, on_device(): weights = jnp.where(allowed, jnp.exp(scores - top), 0.0)  12.9 us
    unnamed x31, local copies, waits for them, and re-layouts  7.34 us
    dot_general x1, matrix products, on_device(): jnp.einsum('htk,khd->thd', probs, near_values, preferred_element_type=jnp...  6.13 us
  transfers between devices with their start and end apart: 5, of which 3 were waited for; matrix products, arithmetic and copies ran while one was open for 17% of the time, Pallas kernels for 0%

commit v1 on v0

v1 whole, which is shorter than its diff:
```python
import functools
import jax
import jax.numpy as jnp
from jax import lax
from jax.experimental import pallas as pl
from jax.experimental.pallas import tpu as pltpu
from jax.sharding import PartitionSpec as P

MESH = pl.DeviceIdType.MESH
NT = (((1,), (1,)), ((), ()))
TN = (((0,), (0,)), ((), ()))
F32 = jnp.float32
BF16 = jnp.bfloat16


def dot(a, b, dims=None):
    if dims is None:
        return jnp.dot(a, b, preferred_element_type=F32)
    return lax.dot_general(a, b, dims, preferred_element_type=F32)


def kernel(n, cell, q_ref, k_ref, v_ref, rates_ref, win_ref, cnt_ref, fast_ref,
           mixed_ref, own_ref,
           r1, r2, cnt1, cnt2, gs, g32, rx, sz, rz, cross, newb, acc, mx, den,
           s1_sem, s2_sem, r1_sem, r2_sem, cs_sem, cr_sem,
           xs_sem, xr_sem, zs_sem, zr_sem, ks_sem, kr_sem,
           as_sem, ar_sem, fs_sem, fr_sem):
    heads, _, fh, dh = fast_ref.shape
    tok = q_ref.shape[0]
    length = tok * n
    me = lax.axis_index("ctx")
    rows = fh // cell
    nz = cell // 2
    cells = n // cell
    base = me // cell * cell
    pos = me % cell
    zc = pos // 2
    xc = pos % 2
    partner = base + 2 * zc + (1 - xc)
    tile = tok // 2

    barrier = pltpu.get_barrier_semaphore()

    @pl.loop(1, n)
    def _(i):
        pl.semaphore_signal(barrier, inc=1, device_id={"ctx": lax.rem(me + i, n)}, device_id_type=MESH)

    pl.semaphore_wait(barrier, n - 1)

    def rdma(src, dst, ssem, rsem, target):
        return pltpu.make_async_remote_copy(
            src_ref=src, dst_ref=dst, send_sem=ssem, recv_sem=rsem,
            device_id={"ctx": target}, device_id_type=MESH)

    kv_refs = (k_ref, v_ref)

    def own_kv(kv, h):
        return kv_refs[kv].at[:, h * dh:(h + 1) * dh]

    def to_two(kv, h):
        return rdma(own_kv(kv, h), r2.at[kv, h], s2_sem.at[kv, h], r2_sem.at[kv, h], me + 2)

    def to_one(kv, h):
        return rdma(own_kv(kv, h), r1.at[kv, h], s1_sem.at[kv, h], r1_sem.at[kv, h], me + 1)

    def relay(kv, h):
        return rdma(r2.at[kv, h], r1.at[kv, h], s1_sem.at[kv, h], r1_sem.at[kv, h], me - 1)

    def count_to(by):
        return rdma(cnt_ref, (cnt1, cnt2)[by - 1], cs_sem.at[by - 1], cr_sem.at[by - 1], me + by)

    even = me % 2 == 0
    relays = jnp.logical_and(me % 2 == 1, me >= 2)

    @pl.when(me + 1 < n)
    def _():
        count_to(1).start()

    @pl.when(me + 2 < n)
    def _():
        count_to(2).start()

    def send_kv(h):
        for kv in range(2):
            @pl.when(me + 2 < n)
            def _():
                to_two(kv, h).start()

            @pl.when(even)
            def _():
                to_one(kv, h).start()

    def relay_kv(h):
        for kv in range(2):
            @pl.when(relays)
            def _():
                to_two(kv, h).wait_recv()
                relay(kv, h).start()

    cnt_own = cnt_ref[0:1, 0:1]
    valid_col = lax.broadcasted_iota(jnp.int32, (tok, 1), 0) < cnt_own
    validf = valid_col.astype(F32)

    def x_copy(h):
        return rdma(gs.at[h, 1 - xc], rx.at[h], xs_sem.at[h], xr_sem.at[h], partner)

    def grads(h):
        cols = slice(h * dh, (h + 1) * dh)
        k = k_ref[:, cols]
        v = v_ref[:, cols]
        h1 = dot(k, fast_ref[h, 0], NT)
        dg = dot(v, fast_ref[h, 1], NT)
        h3 = dot(k, fast_ref[h, 2], NT)
        coef = -(rates_ref[:, h:h + 1] * validf)
        s = jax.nn.sigmoid(h1)
        cs = coef * s
        cdg = cs * dg
        dh1 = (cdg * h3 * (1.0 + h1 * (1.0 - s))).astype(BF16)
        dh3 = (cdg * h1).astype(BF16)
        e2 = (cs * h1 * h3).astype(BF16)
        for m, (left, right) in enumerate(((dh1, k), (e2, v), (dh3, k))):
            g = dot(left, right, TN)
            gb = g.astype(BF16)
            for d in range(cell):
                g32[h, d % 2, d // 2, m] = g[d * rows:(d + 1) * rows]
                gs[h, d % 2, d // 2, m] = gb[d * rows:(d + 1) * rows]
        x_copy(h).start()

    def z_target(i):
        return lax.rem(zc + i, nz)

    def z_send(h, i):
        t = z_target(i)
        return rdma(sz.at[h, t], rz.at[h, i - 1], zs_sem.at[h, i - 1], zr_sem.at[h, i - 1], base + 2 * t + xc)

    def pair_sum(h):
        x_copy(h).wait_recv()
        for z in range(nz):
            total = g32[h, xc, z] + rx[h, z].astype(F32)
            g32[h, xc, z] = total
            sz[h, z] = total.astype(BF16)
        for i in range(1, nz):
            z_send(h, i).start()

    def cross_send(h, i):
        slot = cells - 1 if cells > 1 else 0
        return rdma(cross.at[h, slot], cross.at[h, i - 1], ks_sem.at[h, i - 1], kr_sem.at[h, i - 1],
                    lax.rem(me + i * cell, n))

    def a_copy(h, i):
        block = newb.at[h, pos]
        return rdma(block, block, as_sem.at[h, i - 1], ar_sem.at[h, i - 1], base + 2 * z_target(i) + xc)

    def a_recv(h, i):
        src = lax.rem(zc + nz - i, nz)
        block = newb.at[h, 2 * src + xc]
        return rdma(block, block, as_sem.at[h, i - 1], ar_sem.at[h, i - 1], base + 2 * z_target(i) + xc)

    def f_copy(h, i):
        src = lax.rem(zc + nz - i, nz)
        block = newb.at[h, 2 * src + xc]
        return rdma(block, block, fs_sem.at[h, i], fr_sem.at[h, i], partner)

    def f_recv(h, i):
        src = lax.rem(zc + nz - i, nz)
        block = newb.at[h, 2 * src + 1 - xc]
        return rdma(block, block, fs_sem.at[h, i], fr_sem.at[h, i], partner)

    def norm(h):
        total = g32[h, xc, zc]
        for i in range(1, nz):
            z_send(h, i).wait_recv()
            total = total + rz[h, i - 1].astype(F32)
        if cells > 1:
            cross[h, cells - 1] = total.astype(BF16)
            g32[h, xc, zc] = total

            @pl.loop(1, cells)
            def _(i):
                cross_send(h, i).start()

            @pl.loop(1, cells)
            def _(i):
                cross_send(h, i).wait_recv()
                g32[h, xc, zc] = g32[h, xc, zc] + cross[h, i - 1].astype(F32)

            total = g32[h, xc, zc]
        old = fast_ref[h, :, pl.ds(pl.multiple_of(pos * rows, rows), rows), :].astype(F32)
        upd = old - total * length ** (-0.5)
        scale = lax.rsqrt(jnp.mean(upd * upd, axis=-1, keepdims=True) + 1e-06) * dh ** (-0.5)
        new = (upd * scale).astype(BF16)
        newb[h, pos] = new
        if cells == 1:
            own_ref[h, 0] = new
        for i in range(1, nz):
            a_copy(h, i).start()
        f_copy(h, 0).start()

    def forward(h):
        for i in range(1, nz):
            a_recv(h, i).wait_recv()
            f_copy(h, i).start()

    def attend(h, seg, t, k, v, j0, cnt, first):
        r = slice(t * tile, (t + 1) * tile)
        nk = k.shape[0]
        q = q_ref[r, h * dh:(h + 1) * dh]
        sc = dot(q, k, NT) * dh ** (-0.5)
        i = lax.broadcasted_iota(jnp.int32, (tile, nk), 0) + t * tile
        j = lax.broadcasted_iota(jnp.int32, (tile, nk), 1) + j0
        kv = (lax.broadcasted_iota(jnp.int32, (1, nk), 1) + j0) < cnt
        diff = i - j + seg * tok
        ok = (diff < win_ref[h]) & kv
        if seg == 0:
            ok = ((diff >= 0) & kv) | (diff == 0)
        sc = jnp.where(ok, sc, -1e30)
        top = jnp.max(sc, axis=1, keepdims=True)
        if first:
            p = jnp.exp(sc - top)
            mx[h, r] = top
            den[h, r] = jnp.sum(p, axis=1, keepdims=True)
            acc[h, r] = dot(p.astype(BF16), v)
        else:
            old = mx[h, r]
            top = jnp.maximum(old, top)
            p = jnp.exp(sc - top)
            fix = jnp.exp(old - top)
            mx[h, r] = top
            den[h, r] = den[h, r] * fix + jnp.sum(p, axis=1, keepdims=True)
            acc[h, r] = acc[h, r] * fix + dot(p.astype(BF16), v)

    def own_attend(h):
        cols = slice(h * dh, (h + 1) * dh)
        attend(h, 0, 0, k_ref[:tile, cols], v_ref[:tile, cols], 0, cnt_own, True)
        attend(h, 0, 1, k_ref[:, cols], v_ref[:, cols], 0, cnt_own, True)

    def two_attend(h):
        @pl.when(me >= 2)
        def _():
            @pl.when(even)
            def _():
                for kv in range(2):
                    to_two(kv, h).wait_recv()
            if h == 0:
                count_to(2).wait_recv()
            cnt = cnt2[0:1, 0:1]
            attend(h, 2, 0, r2[0, h], r2[1, h], 0, cnt, False)
            attend(h, 2, 1, r2[0, h, tile:], r2[1, h, tile:], tile, cnt, False)

    def one_attend(h):
        @pl.when(me >= 1)
        def _():
            for kv in range(2):
                to_one(kv, h).wait_recv()
            if h == 0:
                count_to(1).wait_recv()
            cnt = cnt1[0:1, 0:1]
            for t in range(2):
                attend(h, 1, t, r1[0, h], r1[1, h], 0, cnt, False)

    def apply(h):
        for i in range(nz):
            f_recv(h, i).wait_recv()
        w = [newb[h, :, m].reshape(fh, dh) for m in range(3)]
        for t in range(2):
            r = slice(t * tile, (t + 1) * tile)
            cols = slice(h * dh, (h + 1) * dh)
            q = q_ref[r, cols]
            a1 = dot(q, w[0], NT)
            a3 = dot(q, w[2], NT)
            ga = (a1 * jax.nn.sigmoid(a1) * a3).astype(BF16)
            ttt = dot(ga, w[1]) * fh ** (-0.5)
            attn = acc[h, r] / den[h, r]
            mixed_ref[r, cols] = jnp.where(valid_col[r], attn + ttt, 0.0).astype(BF16)

    send_kv(0)
    grads(0)
    grads(1)
    send_kv(1)
    own_attend(0)
    pair_sum(0)
    pair_sum(1)
    own_attend(1)
    norm(0)
    relay_kv(0)
    norm(1)
    forward(0)
    two_attend(0)
    forward(1)
    relay_kv(1)
    one_attend(0)
    two_attend(1)
    apply(0)
    one_attend(1)
    apply(1)

    for by in (1, 2):
        @pl.when(me + by < n)
        def _():
            count_to(by).wait_send()
    for h in range(heads):
        for kv in range(2):
            @pl.when(me + 2 < n)
            def _():
                to_two(kv, h).wait_send()

            @pl.when(even)
            def _():
                to_one(kv, h).wait_send()

            @pl.when(relays)
            def _():
                relay(kv, h).wait_send()
        x_copy(h).wait_send()
        for i in range(1, nz):
            z_send(h, i).wait_send()
            a_copy(h, i).wait_send()
        for i in range(nz):
            f_copy(h, i).wait_send()
        if cells > 1:
            @pl.loop(1, cells)
            def _(i):
                cross_send(h, i).wait_send()
            own_ref[h] = newb[h]


def on_device(n, queries, keys, values, rates, windows, counts, fast):
    tok, width = queries.shape
    fh, heads, mats, dh = fast.shape
    cell = min(n, 8)
    nz = cell // 2
    cells = n // cell
    rows = fh // cell
    rates_t = rates.T
    cnt = jnp.broadcast_to(counts[:, None], (8, 128))
    fast_t = jnp.transpose(fast, (1, 2, 0, 3))
    vmem = pl.BlockSpec(memory_space=pltpu.VMEM)
    smem = pl.BlockSpec(memory_space=pltpu.SMEM)
    blocks = 1 if cells == 1 else cell
    dma = pltpu.SemaphoreType.DMA
    near = max(nz - 1, 1)
    far = max(cells - 1, 1)
    mixed, own = pl.pallas_call(
        functools.partial(kernel, n, cell),
        out_shape=(
            jax.ShapeDtypeStruct((tok, width), BF16),
            jax.ShapeDtypeStruct((heads, blocks, mats, rows, dh), BF16),
        ),
        in_specs=[vmem, vmem, vmem, vmem, smem, vmem, vmem],
        out_specs=(vmem, vmem),
        scratch_shapes=[
            pltpu.VMEM((2, heads, tok, dh), BF16),
            pltpu.VMEM((2, heads, tok, dh), BF16),
            pltpu.VMEM((8, 128), jnp.int32),
            pltpu.VMEM((8, 128), jnp.int32),
            pltpu.VMEM((heads, 2, nz, mats, rows, dh), BF16),
            pltpu.VMEM((heads, 2, nz, mats, rows, dh), F32),
            pltpu.VMEM((heads, nz, mats, rows, dh), BF16),
            pltpu.VMEM((heads, nz, mats, rows, dh), BF16),
            pltpu.VMEM((heads, near, mats, rows, dh), BF16),
            pltpu.VMEM((heads, cells, mats, rows, dh) if cells > 1 else (1, 1, 1, 16, 128), BF16),
            pltpu.VMEM((heads, cell, mats, rows, dh), BF16),
            pltpu.VMEM((heads, tok, dh), F32),
            pltpu.VMEM((heads, tok, 1), F32),
            pltpu.VMEM((heads, tok, 1), F32),
            dma((2, heads)), dma((2, heads)), dma((2, heads)), dma((2, heads)),
            dma((2,)), dma((2,)),
            dma((heads,)), dma((heads,)),
            dma((heads, near)), dma((heads, near)),
            dma((heads, far)), dma((heads, far)),
            dma((heads, near)), dma((heads, near)),
            dma((heads, nz)), dma((heads, nz)),
        ],
        compiler_params=pltpu.CompilerParams(
            collective_id=0, has_side_effects=True, vmem_limit_bytes=50 * 2**20
        ),
    )(queries, keys, values, rates_t, windows, cnt, fast_t)
    if cells == 1:
        new_own = jnp.transpose(own[:, 0], (2, 0, 1, 3))
    else:
        full = jnp.transpose(own, (1, 3, 0, 2, 4)).reshape(fh, heads, mats, dh)
        share = fh // n
        new_own = lax.dynamic_slice_in_dim(full, lax.axis_index("ctx") * share, share, 0)
    return (mixed, new_own)


def solution(mesh):
    in_specs = (
        P(("groups", "ctx"), "head"),
        P(("groups", "ctx"), "head"),
        P(("groups", "ctx"), "head"),
        P("head", ("groups", "ctx")),
        P(("groups", "head")),
        P(("groups", "ctx")),
        P(None, "head", None, None),
    )
    out_specs = (P(("groups", "ctx"), "head"), P(("groups", "ctx"), "head", None, None))
    return jax.shard_map(
        functools.partial(on_device, mesh.shape["ctx"]),
        mesh=mesh, in_specs=in_specs, out_specs=out_specs, check_vma=False
    )
```

time: 218 us -> 131 us (0.60); the launches traced: 214 us -> 130 us
  Pallas kernels: 0 us -> 123 us
  waiting for transfers between devices: 64.2 us -> 0 us
  blocking collectives: 45 us -> 0 us
  starting transfers between devices: 35.8 us -> 0 us
  matrix products: 25.9 us -> 0 us
  other arithmetic: 14.8 us -> 0 us
  between operations: 14.9 us -> 1.33 us
  local copies, waits for them, and re-layouts: 13.3 us -> 5.69 us
    pallas_call x0 -> x1, Pallas kernels: none -> 123 us  [on_device(): pl.pallas_call(functools.partial(kernel, n, cell), out_shape=(jax.ShapeDt...]
    ppermute x4 -> x0, waiting for transfers between devices: 46.7 us -> none  [passed_along(): return lax.ppermute(x, axis, pairs)]
    unnamed x1 -> x0, blocking collectives: 45 us -> none
    ppermute x4 -> x0, starting transfers between devices: 35.7 us -> none  [passed_along(): return lax.ppermute(x, axis, pairs)]
    psum x1 -> x0, waiting for transfers between devices: 17.5 us -> none  [on_device(): grads = lax.psum(jnp.stack([g_one, g_two, g_three], axis=2), 'ctx')]
    dot_general x9 -> x0, matrix products: 13 us -> none  [the longest x1 6.13 us: on_device(): jnp.einsum('htk,khd->thd', probs, near_values, preferred_element_type=jnp...]
    sub x1 -> x0, matrix products: 12.9 us -> none  [on_device(): weights = jnp.where(allowed, jnp.exp(scores - top), 0.0)]
    concatenate x2 -> x0, other arithmetic: 5.4 us -> none  [the longest x1 3.19 us: on_device(): jnp.concatenate(key_list, axis=0).reshape((span + 1) * tok, heads_here, dh)]
  transfers between devices with their start and end apart: 5 -> 0, of which waited for: 3 -> 0; matrix products, arithmetic and copies ran while one was open for 17% -> 0% of each run, Pallas kernels for 0% -> 0%
where the time goes in v1:
time: 131 us; the launch traced here: 130 us
  Pallas kernels  123 us (94%)
  local copies, waits for them, and re-layouts  5.69 us (4%)
  between operations  1.33 us (1%)
    pallas_call x1, Pallas kernels, on_device(): pl.pallas_call(functools.partial(kernel, n, cell), out_shape=(jax.ShapeDt...  123 us
    unnamed x10, local copies, waits for them, and re-layouts  5.69 us

profile of v1, /device:TPU:28, one launch (start us, length us, event | category | flops | bytes accessed | tf_op | source)
XLA Modules:
  0.0 130.4 jit_solution(17944581508185694475)
XLA Ops:
  1.3 0.8 copy.9
  2.1 0.0 copy-start
  2.1 0.0 copy-start.1
  2.1 0.0 copy-start.2
  2.2 3.0 %copy.13 = bf16[256,2,3,512]{3,0,2,1:T(8,128)(2,1)} copy(bf16[256,2,3,512]{3,1,2,0:T(2,128)(2,1)} %param.13) | data formatting | bytes 3145728 | tf_op args[6]
  5.1 0.0 copy-done
  5.2 0.0 copy-done.1
  5.2 0.0 copy-done.2
  5.2 123.4 %shard_map.86 = (bf16[512,1024]{1,0:T(8,128)(2,1)S(1)}, bf16[2,1,3,32,512]{4,3,2,1,0:T(8,128)(2,1)S(1)}) custom-call(bf16[512,1024]{1,0:T(8,128)(2,1)S(1)} %copy-done, bf16[512,1024]{1,0:T(8,128)(2,1)S(1)} %copy-done.1, bf16[512,1024]{1,0:T(8,128)(2,1)} %v_ref.1, f32[512,2]{1,0:T(8,128)S(1)} %bitcast.9, s32[2]{0:T(128)S(1)} %copy-done.2, ...), custom_call_target="tpu_custom_call" | custom-call | tf_op jit(solution)/shard_map/pallas_call | solution.py:343
  128.6 0.9 copy.11
  129.5 1.0 copy.16
  (1 shorter events, 0.0 us)
Async XLA Ops:
  2.1 3.0 %copy-start = (bf16[512,1024]{1,0:T(8,128)(2,1)S(1)}, bf16[512,1024]{1,0:T(8,128)(2,1)}, u32[]{:S(2)}) copy-start(bf16[512,1024]{1,0:T(8,128)(2,1)} %q_ref.1) | copy-start | bytes 3145732
  2.1 3.0 %copy-start.1 = (bf16[512,1024]{1,0:T(8,128)(2,1)S(1)}, bf16[512,1024]{1,0:T(8,128)(2,1)}, u32[]{:S(2)}) copy-start(bf16[512,1024]{1,0:T(8,128)(2,1)} %k_ref.1) | copy-start | bytes 3145732
  2.1 3.0 %copy-start.2 = (s32[2]{0:T(128)S(1)}, s32[2]{0:T(128)}, u32[]{:S(2)}) copy-start(s32[2]{0:T(128)} %win_ref.1) | copy-start | bytes 28

commit v2 on v0

v2 whole, which is shorter than its diff:
```python
import functools
import jax
import jax.numpy as jnp
from jax import lax
from jax.experimental import pallas as pl
from jax.experimental.pallas import tpu as pltpu
from jax.sharding import PartitionSpec as P

MESH = pl.DeviceIdType.MESH
NT = (((1,), (1,)), ((), ()))
TN = (((0,), (0,)), ((), ()))
F32 = jnp.float32
BF16 = jnp.bfloat16


def dot(a, b, dims=None):
    if dims is None:
        return jnp.dot(a, b, preferred_element_type=F32)
    return lax.dot_general(a, b, dims, preferred_element_type=F32)


def kernel(n, cell, q_ref, k_ref, v_ref, meta_ref, win_ref, fast_ref,
           mixed_ref, own_ref,
           kvq, prev, metas, gs, g32, rz, cross, newb, xbuf, acc, mx, den, ttt, outs, outr,
           x_s, x_r, d_s, d_r, y_s, y_r, m_s, m_r, z_s, z_r, c_s, c_r, a_s, a_r, n_s, n_r, o_s, o_r):
    _, _, fh, dh = fast_ref.shape
    tok = q_ref.shape[0]
    length = tok * n
    me = lax.axis_index("ctx")
    nz = cell // 2
    cells = n // cell
    rows = fh // nz
    half = rows // 2
    base = me // cell * cell
    zc = me % cell // 2
    xc = me % 2
    oc = 1 - xc
    partner = me + 1 - 2 * xc
    tile = tok // 2
    has_prev = me >= 2
    has_next = me + 2 < n

    barrier = pltpu.get_barrier_semaphore()

    @pl.loop(1, n)
    def _(i):
        pl.semaphore_signal(barrier, inc=1, device_id={"ctx": lax.rem(me + i, n)}, device_id_type=MESH)

    pl.semaphore_wait(barrier, n - 1)

    def rdma(src, dst, ssem, rsem, target):
        return pltpu.make_async_remote_copy(
            src_ref=src, dst_ref=dst, send_sem=ssem, recv_sem=rsem,
            device_id={"ctx": target}, device_id_type=MESH)

    refs = (k_ref, v_ref, q_ref)
    mine = pl.ds(pl.multiple_of(xc * dh, dh), dh)
    other = pl.ds(pl.multiple_of(oc * dh, dh), dh)

    def swap(i):
        return rdma(refs[i].at[:, other], kvq.at[i, xc], x_s.at[i], x_r.at[i], partner)

    def direct(i):
        return rdma(refs[i].at[:, mine], prev.at[i, xc], d_s.at[i], d_r.at[i], me + 2)

    def relay(i):
        return rdma(kvq.at[i, oc], prev.at[i, oc], y_s.at[i], y_r.at[i], me + 2)

    def meta_pair():
        return rdma(meta_ref, metas.at[2], m_s.at[0], m_r.at[0], partner)

    def meta_next(same):
        return rdma(meta_ref, metas.at[xc], m_s.at[2 - same], m_r.at[2 - same], (me if same else partner) + 2)

    def z_target(i):
        return base + 2 * lax.rem(zc + i, nz) + xc

    def z_send(i):
        return rdma(gs.at[lax.rem(zc + i, nz)], rz.at[i - 1], z_s.at[i - 1], z_r.at[i - 1], z_target(i))

    def cross_send(i):
        return rdma(cross.at[cells - 1], cross.at[i - 1], c_s.at[i - 1], c_r.at[i - 1], lax.rem(me + i * cell, n))

    def a_send(i):
        return rdma(newb.at[zc], newb.at[zc], a_s.at[i - 1], a_r.at[i - 1], z_target(i))

    def a_recv(i):
        block = newb.at[lax.rem(zc + nz - i, nz)]
        return rdma(block, block, a_s.at[i - 1], a_r.at[i - 1], z_target(i))

    def new_swap():
        if cells == 1:
            part = newb.at[zc, :, pl.ds(pl.multiple_of(oc * half, half), half)]
        else:
            part = newb
        return rdma(part, xbuf, n_s.at[0], n_r.at[0], partner)

    def out_send(t):
        r = pl.ds(t * tile, tile)
        return rdma(outs.at[r], outr.at[r], o_s.at[t], o_r.at[t], partner)

    meta_pair().start()

    @pl.when(has_next)
    def _():
        meta_next(1).start()
        meta_next(0).start()

    for i in range(2):
        swap(i).start()

        @pl.when(has_next)
        def _():
            direct(i).start()
    swap(2).start()

    for i in range(3):
        kvq[i, xc] = refs[i][:, mine]

    window = win_ref[xc]

    def count_of(m):
        return m[2:3, 0:1].astype(jnp.int32)

    def valid_of(cnt):
        return lax.broadcasted_iota(jnp.int32, (tok, 1), 0) < cnt

    cnt_own = count_of(meta_ref)

    def grads(s, meta, first):
        k = kvq[0, s]
        v = kvq[1, s]
        h1 = dot(k, fast_ref[xc, 0], NT)
        dg = dot(v, fast_ref[xc, 1], NT)
        h3 = dot(k, fast_ref[xc, 2], NT)
        turned = jnp.transpose(meta[...])
        rate = jnp.where(xc == 0, turned[:, 0:1], turned[:, 1:2])
        coef = -(rate * valid_of(count_of(meta)).astype(F32))
        sg = jax.nn.sigmoid(h1)
        cs = coef * sg
        cdg = cs * dg
        dh1 = (cdg * h3 * (1.0 + h1 * (1.0 - sg))).astype(BF16)
        dh3 = (cdg * h1).astype(BF16)
        e2 = (cs * h1 * h3).astype(BF16)
        for m, (left, right) in enumerate(((dh1, k), (e2, v), (dh3, k))):
            g = dot(left, right, TN)
            for z in range(nz):
                part = g[z * rows:(z + 1) * rows]
                if first:
                    g32[z, m] = part
                else:
                    part = part + g32[z, m]
                    g32[z, m] = part
                    gs[z, m] = part.astype(BF16)

    def norm():
        total = g32[zc]
        for i in range(1, nz):
            z_send(i).wait_recv()
            total = total + rz[i - 1].astype(F32)
        if cells > 1:
            cross[cells - 1] = total.astype(BF16)
            g32[zc] = total

            @pl.loop(1, cells)
            def _(i):
                cross_send(i).start()

            @pl.loop(1, cells)
            def _(i):
                cross_send(i).wait_recv()
                g32[zc] = g32[zc] + cross[i - 1].astype(F32)

            total = g32[zc]
        old = fast_ref[xc, :, pl.ds(pl.multiple_of(zc * rows, rows), rows), :].astype(F32)
        upd = old - total * length ** (-0.5)
        scale = lax.rsqrt(jnp.mean(upd * upd, axis=-1, keepdims=True) + 1e-06) * dh ** (-0.5)
        newb[zc] = (upd * scale).astype(BF16)
        for i in range(1, nz):
            a_send(i).start()
        if cells == 1:
            new_swap().start()
            own_ref[xc] = newb[zc, :, pl.ds(pl.multiple_of(xc * half, half), half)]

    def attend(qs, seg, t, k, v, j0, cnt):
        r = slice(t * tile, (t + 1) * tile)
        nk = k.shape[0]
        sc = dot(kvq[2, qs, r], k, NT) * dh ** (-0.5)
        i = lax.broadcasted_iota(jnp.int32, (tile, nk), 0) + t * tile
        j = lax.broadcasted_iota(jnp.int32, (tile, nk), 1) + j0
        kv = (lax.broadcasted_iota(jnp.int32, (1, nk), 1) + j0) < cnt
        diff = i - j + seg * tok
        if seg == 0:
            ok = ((diff >= 0) & kv) | (diff == 0)
        else:
            ok = (diff < window) & kv
        sc = jnp.where(ok, sc, -1e30)
        top = jnp.max(sc, axis=1, keepdims=True)
        if seg == 0:
            p = jnp.exp(sc - top)
            mx[qs, r] = top
            den[qs, r] = jnp.sum(p, axis=1, keepdims=True)
            acc[qs, r] = dot(p.astype(BF16), v)
        else:
            old = mx[qs, r]
            top = jnp.maximum(old, top)
            p = jnp.exp(sc - top)
            fix = jnp.exp(old - top)
            mx[qs, r] = top
            den[qs, r] = den[qs, r] * fix + jnp.sum(p, axis=1, keepdims=True)
            acc[qs, r] = acc[qs, r] * fix + dot(p.astype(BF16), v)

    def causal(s, cnt):
        attend(s, 0, 0, kvq[0, s, :tile], kvq[1, s, :tile], 0, cnt)
        attend(s, 0, 1, kvq[0, s], kvq[1, s], 0, cnt)

    def full(qs, k, v, cnt):
        for t in range(2):
            attend(qs, 1, t, k, v, 0, cnt)

    def far(qs, ks, cnt):
        attend(qs, 2, 0, prev[0, ks], prev[1, ks], 0, cnt)
        attend(qs, 2, 1, prev[0, ks, tile:], prev[1, ks, tile:], tile, cnt)

    def prev_step(ks, arrived):
        @pl.when(jnp.logical_and(has_prev, arrived))
        def _():
            cnt = count_of(metas[ks])
            far(ks, ks, cnt)
            if ks == 1:
                full(0, prev[0, 1], prev[1, 1], cnt)

    def apply(s):
        w = [newb[:, m].reshape(fh, dh) for m in range(3)]
        for t in range(2):
            r = slice(t * tile, (t + 1) * tile)
            q = kvq[2, s, r]
            a1 = dot(q, w[0], NT)
            a3 = dot(q, w[2], NT)
            ga = (a1 * jax.nn.sigmoid(a1) * a3).astype(BF16)
            ttt[s, r] = dot(ga, w[1]) * fh ** (-0.5)

    def result(s, cnt, t):
        r = slice(t * tile, (t + 1) * tile)
        return jnp.where(valid_of(cnt)[r], acc[s, r] / den[s, r] + ttt[s, r], 0.0).astype(BF16)

    grads(xc, meta_ref, True)
    causal(xc, cnt_own)
    meta_pair().wait_recv()
    cnt_pair = count_of(metas[2])
    for i in range(2):
        swap(i).wait_recv()
    grads(oc, metas.at[2], False)
    for i in range(1, nz):
        z_send(i).start()

    @pl.when(has_next)
    def _():
        for i in range(2):
            relay(i).start()

    swap(2).wait_recv()
    causal(oc, cnt_pair)
    full(1, kvq[0, 0], kvq[1, 0], jnp.where(xc == 0, cnt_own, cnt_pair))
    norm()

    @pl.when(has_prev)
    def _():
        meta_next(1).wait_recv()
        meta_next(0).wait_recv()
        for i in range(2):
            direct(i).wait_recv()

    prev_step(0, xc == 0)
    prev_step(1, xc == 1)
    for i in range(1, nz):
        a_recv(i).wait_recv()
    apply(0)
    apply(1)

    @pl.when(has_prev)
    def _():
        for i in range(2):
            relay(i).wait_recv()

    prev_step(0, xc == 1)
    prev_step(1, xc == 0)
    for t in range(2):
        outs[t * tile:(t + 1) * tile] = result(oc, cnt_pair, t)
        out_send(t).start()
    for t in range(2):
        mixed_ref[t * tile:(t + 1) * tile, mine] = result(xc, cnt_own, t)
    if cells > 1:
        new_swap().start()
        own_ref[xc] = newb[...]
    new_swap().wait_recv()
    own_ref[oc] = xbuf[...]
    for t in range(2):
        out_send(t).wait_recv()
        mixed_ref[t * tile:(t + 1) * tile, other] = outr[t * tile:(t + 1) * tile]

    meta_pair().wait_send()
    for i in range(3):
        swap(i).wait_send()

    @pl.when(has_next)
    def _():
        meta_next(1).wait_send()
        meta_next(0).wait_send()
        for i in range(2):
            direct(i).wait_send()
            relay(i).wait_send()

    for i in range(1, nz):
        z_send(i).wait_send()
        a_send(i).wait_send()
    new_swap().wait_send()
    for t in range(2):
        out_send(t).wait_send()
    if cells > 1:
        @pl.loop(1, cells)
        def _(i):
            cross_send(i).wait_send()


def on_device(n, queries, keys, values, rates, windows, counts, fast):
    tok, width = queries.shape
    fh, heads, mats, dh = fast.shape
    cell = min(n, 8)
    nz = cell // 2
    cells = n // cell
    rows = fh // nz
    count_row = jnp.broadcast_to(counts[:, None].astype(F32), (8 - heads, tok))
    meta = jnp.concatenate([rates, count_row], axis=0)
    fast_t = jnp.transpose(fast, (1, 2, 0, 3))
    vmem = pl.BlockSpec(memory_space=pltpu.VMEM)
    smem = pl.BlockSpec(memory_space=pltpu.SMEM)
    share = (mats, rows // 2, dh) if cells == 1 else (nz, mats, rows, dh)
    dma = pltpu.SemaphoreType.DMA
    near = max(nz - 1, 1)
    mixed, own = pl.pallas_call(
        functools.partial(kernel, n, cell),
        out_shape=(
            jax.ShapeDtypeStruct((tok, width), BF16),
            jax.ShapeDtypeStruct((heads,) + share, BF16),
        ),
        in_specs=[vmem, vmem, vmem, vmem, smem, vmem],
        out_specs=(vmem, vmem),
        scratch_shapes=[
            pltpu.VMEM((3, 2, tok, dh), BF16),
            pltpu.VMEM((2, 2, tok, dh), BF16),
            pltpu.VMEM((3, 8, tok), F32),
            pltpu.VMEM((nz, mats, rows, dh), BF16),
            pltpu.VMEM((nz, mats, rows, dh), F32),
            pltpu.VMEM((near, mats, rows, dh), BF16),
            pltpu.VMEM((cells, mats, rows, dh) if cells > 1 else (1, 1, 16, 128), BF16),
            pltpu.VMEM((nz, mats, rows, dh), BF16),
            pltpu.VMEM(share, BF16),
            pltpu.VMEM((2, tok, dh), F32),
            pltpu.VMEM((2, tok, 1), F32),
            pltpu.VMEM((2, tok, 1), F32),
            pltpu.VMEM((2, tok, dh), F32),
            pltpu.VMEM((tok, dh), BF16),
            pltpu.VMEM((tok, dh), BF16),
            dma((3,)), dma((3,)), dma((2,)), dma((2,)), dma((2,)), dma((2,)),
            dma((3,)), dma((3,)), dma((near,)), dma((near,)),
            dma((max(cells - 1, 1),)), dma((max(cells - 1, 1),)),
            dma((near,)), dma((near,)), dma((1,)), dma((1,)), dma((2,)), dma((2,)),
        ],
        compiler_params=pltpu.CompilerParams(
            collective_id=0, has_side_effects=True, vmem_limit_bytes=50 * 2**20
        ),
    )(queries, keys, values, meta, windows, fast_t)
    if cells == 1:
        new_own = jnp.transpose(own, (2, 0, 1, 3))
    else:
        full = jnp.transpose(own, (1, 3, 0, 2, 4)).reshape(fh, heads, mats, dh)
        part = fh // n
        new_own = lax.dynamic_slice_in_dim(full, lax.axis_index("ctx") * part, part, 0)
    return (mixed, new_own)


def solution(mesh):
    in_specs = (
        P(("groups", "ctx"), "head"),
        P(("groups", "ctx"), "head"),
        P(("groups", "ctx"), "head"),
        P("head", ("groups", "ctx")),
        P(("groups", "head")),
        P(("groups", "ctx")),
        P(None, "head", None, None),
    )
    out_specs = (P(("groups", "ctx"), "head"), P(("groups", "ctx"), "head", None, None))
    return jax.shard_map(
        functools.partial(on_device, mesh.shape["ctx"]),
        mesh=mesh, in_specs=in_specs, out_specs=out_specs, check_vma=False
    )
```

time: 218 us -> 109 us (0.50); the launches traced: 214 us -> 108 us
  Pallas kernels: 0 us -> 101 us
  waiting for transfers between devices: 64.2 us -> 0 us
  blocking collectives: 45 us -> 0 us
  starting transfers between devices: 35.8 us -> 0 us
  matrix products: 25.9 us -> 0 us
  other arithmetic: 14.8 us -> 0 us
  between operations: 14.9 us -> 1.3 us
  local copies, waits for them, and re-layouts: 13.3 us -> 5.55 us
    pallas_call x0 -> x1, Pallas kernels: none -> 101 us  [on_device(): pl.pallas_call(functools.partial(kernel, n, cell), out_shape=(jax.ShapeDt...]
    ppermute x4 -> x0, waiting for transfers between devices: 46.7 us -> none  [passed_along(): return lax.ppermute(x, axis, pairs)]
    unnamed x1 -> x0, blocking collectives: 45 us -> none
    ppermute x4 -> x0, starting transfers between devices: 35.7 us -> none  [passed_along(): return lax.ppermute(x, axis, pairs)]
    psum x1 -> x0, waiting for transfers between devices: 17.5 us -> none  [on_device(): grads = lax.psum(jnp.stack([g_one, g_two, g_three], axis=2), 'ctx')]
    dot_general x9 -> x0, matrix products: 13 us -> none  [the longest x1 6.13 us: on_device(): jnp.einsum('htk,khd->thd', probs, near_values, preferred_element_type=jnp...]
    sub x1 -> x0, matrix products: 12.9 us -> none  [on_device(): weights = jnp.where(allowed, jnp.exp(scores - top), 0.0)]
    concatenate x2 -> x0, other arithmetic: 5.4 us -> none  [the longest x1 3.19 us: on_device(): jnp.concatenate(key_list, axis=0).reshape((span + 1) * tok, heads_here, dh)]
  transfers between devices with their start and end apart: 5 -> 0, of which waited for: 3 -> 0; matrix products, arithmetic and copies ran while one was open for 17% -> 0% of each run, Pallas kernels for 0% -> 0%
where the time goes in v2:
time: 109 us; the launch traced here: 108 us
  Pallas kernels  101 us (93%)
  local copies, waits for them, and re-layouts  5.55 us (5%)
  between operations  1.3 us (1%)
    pallas_call x1, Pallas kernels, on_device(): pl.pallas_call(functools.partial(kernel, n, cell), out_shape=(jax.ShapeDt...  101 us
    unnamed x9, local copies, waits for them, and re-layouts  4.85 us

profile of v2, /device:TPU:28, one launch (start us, length us, event | category | flops | bytes accessed | tf_op | source)
XLA Modules:
  0.0 108.2 jit_solution(15853383293965881911)
XLA Ops:
  1.3 0.7 concatenate.3.meta_ref
  2.0 0.0 copy-start
  2.0 0.0 copy-start.1
  2.0 0.0 copy-start.2
  2.0 3.0 %copy.12 = bf16[256,2,3,512]{3,0,2,1:T(8,128)(2,1)} copy(bf16[256,2,3,512]{3,1,2,0:T(2,128)(2,1)} %param.13) | data formatting | bytes 3145728 | tf_op args[6]
  5.0 0.0 copy-done
  5.0 0.0 copy-done.1
  5.0 0.0 copy-done.2
  5.0 101.3 %shard_map.86 = (bf16[512,1024]{1,0:T(8,128)(2,1)S(1)}, bf16[2,3,32,512]{3,2,1,0:T(8,128)(2,1)S(1)}) custom-call(bf16[512,1024]{1,0:T(8,128)(2,1)S(1)} %copy-done, bf16[512,1024]{1,0:T(8,128)(2,1)S(1)} %copy-done.1, bf16[512,1024]{1,0:T(8,128)(2,1)} %v_ref.1, f32[8,512]{1,0:T(8,128)S(1)} %concatenate.3.meta_ref, s32[2]{0:T(128)S(1)} %copy-done.2, ...), custom_call_target="tpu_custom_call" | custom-call | tf_op jit(solution)/shard_map/pallas_call | solution.py:341
  106.3 0.9 copy.10
  107.2 1.0 copy.15
Async XLA Ops:
  2.0 3.0 %copy-start = (bf16[512,1024]{1,0:T(8,128)(2,1)S(1)}, bf16[512,1024]{1,0:T(8,128)(2,1)}, u32[]{:S(2)}) copy-start(bf16[512,1024]{1,0:T(8,128)(2,1)} %q_ref.1) | copy-start | bytes 3145732
  2.0 3.0 %copy-start.1 = (bf16[512,1024]{1,0:T(8,128)(2,1)S(1)}, bf16[512,1024]{1,0:T(8,128)(2,1)}, u32[]{:S(2)}) copy-start(bf16[512,1024]{1,0:T(8,128)(2,1)} %k_ref.1) | copy-start | bytes 3145732
  2.0 3.0 %copy-start.2 = (s32[2]{0:T(128)S(1)}, s32[2]{0:T(128)}, u32[]{:S(2)}) copy-start(s32[2]{0:T(128)} %win_ref.1) | copy-start | bytes 28

commit v3 on v2

--- a/solution.py
+++ b/solution.py
@@ -72,21 +72,18 @@
     def meta_next(same):
         return rdma(meta_ref, metas.at[xc], m_s.at[2 - same], m_r.at[2 - same], (me if same else partner) + 2)
 
-    def z_target(i):
-        return base + 2 * lax.rem(zc + i, nz) + xc
-
-    def z_send(i):
-        return rdma(gs.at[lax.rem(zc + i, nz)], rz.at[i - 1], z_s.at[i - 1], z_r.at[i - 1], z_target(i))
+    def near_z(up):
+        return me + 2 if up else me - 2
+
+    def sum_send(up, t):
+        return rdma(gs.at[t], rz.at[up, t], z_s.at[up, t], z_r.at[up, t], near_z(up))
 
     def cross_send(i):
         return rdma(cross.at[cells - 1], cross.at[i - 1], c_s.at[i - 1], c_r.at[i - 1], lax.rem(me + i * cell, n))
 
-    def a_send(i):
-        return rdma(newb.at[zc], newb.at[zc], a_s.at[i - 1], a_r.at[i - 1], z_target(i))
-
-    def a_recv(i):
-        block = newb.at[lax.rem(zc + nz - i, nz)]
-        return rdma(block, block, a_s.at[i - 1], a_r.at[i - 1], z_target(i))
+    def row_send(up, d, block):
+        b = newb.at[block]
+        return rdma(b, b, a_s.at[up, d], a_r.at[up, d], near_z(up))
 
     def new_swap():
         if cells == 1:
@@ -112,7 +109,6 @@
         @pl.when(has_next)
         def _():
             direct(i).start()
-    swap(2).start()
 
     for i in range(3):
         kvq[i, xc] = refs[i][:, mine]
@@ -151,13 +147,36 @@
                 else:
                     part = part + g32[z, m]
                     g32[z, m] = part
-                    gs[z, m] = part.astype(BF16)
+
+    def sum_step(up, t):
+        @pl.when(zc < t if up else zc > t)
+        def _():
+            inner = zc > 0 if up else zc < nz - 1
+
+            @pl.when(inner)
+            def _():
+                sum_send(up, t).wait_recv()
+                gs[t] = (g32[t] + rz[up, t].astype(F32)).astype(BF16)
+
+            @pl.when(jnp.logical_not(inner))
+            def _():
+                gs[t] = g32[t].astype(BF16)
+
+            sum_send(up, t).start()
+
+    def sums():
+        for i in range(nz - 1):
+            sum_step(1, nz - 1 - i)
+            sum_step(0, i)
 
     def norm():
+        for up in (1, 0):
+            @pl.when(zc > 0 if up else zc < nz - 1)
+            def _():
+                sum_send(up, zc).wait_recv()
+                g32[zc] = g32[zc] + rz[up, zc].astype(F32)
+
         total = g32[zc]
-        for i in range(1, nz):
-            z_send(i).wait_recv()
-            total = total + rz[i - 1].astype(F32)
         if cells > 1:
             cross[cells - 1] = total.astype(BF16)
             g32[zc] = total
@@ -176,11 +195,26 @@
         upd = old - total * length ** (-0.5)
         scale = lax.rsqrt(jnp.mean(upd * upd, axis=-1, keepdims=True) + 1e-06) * dh ** (-0.5)
         newb[zc] = (upd * scale).astype(BF16)
-        for i in range(1, nz):
-            a_send(i).start()
+        for up in (1, 0):
+            @pl.when(zc < nz - 1 if up else zc > 0)
+            def _():
+                row_send(up, 0, zc).start()
+
         if cells == 1:
             new_swap().start()
             own_ref[xc] = newb[zc, :, pl.ds(pl.multiple_of(xc * half, half), half)]
+
+    def gather(d):
+        for up in (1, 0):
+            block = zc - d if up else zc + d
+
+            @pl.when(block >= 0 if up else block < nz)
+            def _():
+                row_send(up, d - 1, block).wait_recv()
+
+                @pl.when(zc < nz - 1 if up else zc > 0)
+                def _():
+                    row_send(up, d, block).start()
 
     def attend(qs, seg, t, k, v, j0, cnt):
         r = slice(t * tile, (t + 1) * tile)
@@ -250,20 +284,23 @@
     cnt_pair = count_of(metas[2])
     for i in range(2):
         swap(i).wait_recv()
+    swap(2).start()
     grads(oc, metas.at[2], False)
-    for i in range(1, nz):
-        z_send(i).start()
 
     @pl.when(has_next)
     def _():
-        for i in range(2):
-            relay(i).start()
-
+        relay(0).start()
+
+    sums()
     swap(2).wait_recv()
     causal(oc, cnt_pair)
     full(1, kvq[0, 0], kvq[1, 0], jnp.where(xc == 0, cnt_own, cnt_pair))
     norm()
 
+    @pl.when(has_next)
+    def _():
+        relay(1).start()
+
     @pl.when(has_prev)
     def _():
         meta_next(1).wait_recv()
@@ -271,10 +308,12 @@
         for i in range(2):
             direct(i).wait_recv()
 
+    if nz > 1:
+        gather(1)
     prev_step(0, xc == 0)
     prev_step(1, xc == 1)
-    for i in range(1, nz):
-        a_recv(i).wait_recv()
+    for d in range(2, nz):
+        gather(d)
     apply(0)
     apply(1)
 
@@ -311,9 +350,19 @@
             direct(i).wait_send()
             relay(i).wait_send()
 
-    for i in range(1, nz):
-        z_send(i).wait_send()
-        a_send(i).wait_send()
+    for up in (1, 0):
+        for t in range(nz):
+            @pl.when(zc < t if up else zc > t)
+            def _():
+                sum_send(up, t).wait_send()
+
+        for d in range(nz - 1):
+            block = zc - d if up else zc + d
+
+            @pl.when(jnp.logical_and(block >= 0, zc < nz - 1) if up else jnp.logical_and(block < nz, zc > 0))
+            def _():
+                row_send(up, d, block).wait_send()
+
     new_swap().wait_send()
     for t in range(2):
         out_send(t).wait_send()
@@ -337,7 +386,6 @@
     smem = pl.BlockSpec(memory_space=pltpu.SMEM)
     share = (mats, rows // 2, dh) if cells == 1 else (nz, mats, rows, dh)
     dma = pltpu.SemaphoreType.DMA
-    near = max(nz - 1, 1)
     mixed, own = pl.pallas_call(
         functools.partial(kernel, n, cell),
         out_shape=(
@@ -352,7 +400,7 @@
             pltpu.VMEM((3, 8, tok), F32),
             pltpu.VMEM((nz, mats, rows, dh), BF16),
             pltpu.VMEM((nz, mats, rows, dh), F32),
-            pltpu.VMEM((near, mats, rows, dh), BF16),
+            pltpu.VMEM((2, nz, mats, rows, dh), BF16),
             pltpu.VMEM((cells, mats, rows, dh) if cells > 1 else (1, 1, 16, 128), BF16),
             pltpu.VMEM((nz, mats, rows, dh), BF16),
             pltpu.VMEM(share, BF16),
@@ -363,9 +411,9 @@
             pltpu.VMEM((tok, dh), BF16),
             pltpu.VMEM((tok, dh), BF16),
             dma((3,)), dma((3,)), dma((2,)), dma((2,)), dma((2,)), dma((2,)),
-            dma((3,)), dma((3,)), dma((near,)), dma((near,)),
+            dma((3,)), dma((3,)), dma((2, nz)), dma((2, nz)),
             dma((max(cells - 1, 1),)), dma((max(cells - 1, 1),)),
-            dma((near,)), dma((near,)), dma((1,)), dma((1,)), dma((2,)), dma((2,)),
+            dma((2, nz)), dma((2, nz)), dma((1,)), dma((1,)), dma((2,)), dma((2,)),
         ],
         compiler_params=pltpu.CompilerParams(
             collective_id=0, has_side_effects=True, vmem_limit_bytes=50 * 2**20

time: 109 us -> 105 us (0.963)
  Pallas kernels: 101 us -> 97.1 us
    pallas_call x1, Pallas kernels: 101 us -> 97.1 us  [on_device(): pl.pallas_call(functools.partial(kernel, n, cell), out_shape=(jax.ShapeDt...]
where the time goes in v3:
time: 105 us; the launch traced here: 104 us
  Pallas kernels  97.1 us (92%)
  local copies, waits for them, and re-layouts  5.55 us (5%)
  between operations  1.3 us (1%)
    pallas_call x1, Pallas kernels, on_device(): pl.pallas_call(functools.partial(kernel, n, cell), out_shape=(jax.ShapeDt...  97.1 us
    unnamed x9, local copies, waits for them, and re-layouts  4.85 us

profile of v3, /device:TPU:28, one launch (start us, length us, event | category | flops | bytes accessed | tf_op | source)
XLA Modules:
  0.0 104.0 jit_solution(6701255008007799873)
XLA Ops:
  1.3 0.7 concatenate.3.meta_ref
  2.0 0.0 copy-start
  2.0 0.0 copy-start.1
  2.0 0.0 copy-start.2
  2.0 3.0 %copy.12 = bf16[256,2,3,512]{3,0,2,1:T(8,128)(2,1)} copy(bf16[256,2,3,512]{3,1,2,0:T(2,128)(2,1)} %param.13) | data formatting | bytes 3145728 | tf_op args[6]
  5.0 0.0 copy-done
  5.0 0.0 copy-done.1
  5.0 0.0 copy-done.2
  5.0 97.1 %shard_map.86 = (bf16[512,1024]{1,0:T(8,128)(2,1)S(1)}, bf16[2,3,32,512]{3,2,1,0:T(8,128)(2,1)S(1)}) custom-call(bf16[512,1024]{1,0:T(8,128)(2,1)S(1)} %copy-done, bf16[512,1024]{1,0:T(8,128)(2,1)S(1)} %copy-done.1, bf16[512,1024]{1,0:T(8,128)(2,1)} %v_ref.1, f32[8,512]{1,0:T(8,128)S(1)} %concatenate.3.meta_ref, s32[2]{0:T(128)S(1)} %copy-done.2, ...), custom_call_target="tpu_custom_call" | custom-call | tf_op jit(solution)/shard_map/pallas_call | solution.py:389
  102.1 0.9 copy.10
  103.0 1.0 copy.15
Async XLA Ops:
  2.0 3.0 %copy-start = (bf16[512,1024]{1,0:T(8,128)(2,1)S(1)}, bf16[512,1024]{1,0:T(8,128)(2,1)}, u32[]{:S(2)}) copy-start(bf16[512,1024]{1,0:T(8,128)(2,1)} %q_ref.1) | copy-start | bytes 3145732
  2.0 3.0 %copy-start.1 = (bf16[512,1024]{1,0:T(8,128)(2,1)S(1)}, bf16[512,1024]{1,0:T(8,128)(2,1)}, u32[]{:S(2)}) copy-start(bf16[512,1024]{1,0:T(8,128)(2,1)} %k_ref.1) | copy-start | bytes 3145732
  2.0 3.0 %copy-start.2 = (s32[2]{0:T(128)S(1)}, s32[2]{0:T(128)}, u32[]{:S(2)}) copy-start(s32[2]{0:T(128)} %win_ref.1) | copy-start | bytes 28
